TPU v7x, 256 devices: a whole 4x4x8 slice. The times are simulated.
256 devices in a mesh: group: 4 (over x), dev: 64 (over y, z, core).
Axes of the slice: x: 4, y: 4, z: 8, core: 2. Of those that a mesh axis runs over, the one named last changes fastest.
Arguments:
- node_aggregate: bfloat16 [16384, 512], P(('group', 'dev')), may hold values from -6 to 6
- weight: bfloat16 [512, 512], replicated, may hold values from -0.25 to 0.25
- tiles: bfloat16 [8192, 128, 128], P(('group', 'dev'))
- tile_src: int32 [8192], P(('group', 'dev')), may hold values from 0 to 31
- tile_dst: int32 [8192], P(('group', 'dev')), may hold values from 0 to 1
- tile_count: int32 [256], P(('group', 'dev')), may hold values from 8 to 32
- pair_owner: int32 [2097152, 2], P(('group', 'dev')), may hold values from 0 to 63, all different within a row; in each aligned block of 8192 rows (0 to 8191, 8192 to 16383, ...) at most 512 rows name the same one
- pair_row: int32 [2097152, 2], P(('group', 'dev')), may hold values from 0 to 63
Outputs:
- feature_grad: bfloat16 [16384, 512], P(('group', 'dev'))
- weight_grad: float32 [512, 512], replicated
Inputs may be any that keep to these rules, and one draw needn't show every extreme that they name: `pair_owner`: among the 16384 pair ends held by one device, at most 512 name one owner, and the two ends of a pair name different owners.
All inputs are finite; a program needn't handle non-finite values.
Results may differ from a plain program's by a relative error of at most 0.0032.
The roundings to bfloat16 on the way count: a program that leaves them out, or rounds other values in their place, can miss the bound.
Values may be sent and summed in bfloat16 or wider, within the bound.
No kernel may reach another device: no remote copies, remote signals or barrier semaphores. Data moves between devices by JAX's collectives and lax.ppermute only.
A program may use at most 128 MiB of HBM per device.

v0:
```python
import math
import jax
import jax.numpy as jnp
from jax import lax
from jax.sharding import PartitionSpec as P


def activation(values):
    return jax.nn.gelu(values)


def per_device(node_aggregate, weight, tiles, tile_src, tile_dst, tile_count, pair_owner, pair_row):
    master_rows, feature_width = node_aggregate.shape
    tile_size = tiles.shape[1]
    pre_act = jnp.dot(node_aggregate, weight, preferred_element_type=jnp.float32)
    hidden, act_back = jax.vjp(activation, pre_act)
    hidden_b = hidden.astype(jnp.bfloat16)
    mirror = lax.all_gather(hidden_b, "dev", axis=0, tiled=True)
    pair_total = pair_owner.shape[0]
    node_a = pair_owner[:, 0] * master_rows + pair_row[:, 0]
    node_b = pair_owner[:, 1] * master_rows + pair_row[:, 1]
    head_rows = mirror[node_a]
    tail_rows = mirror[node_b]
    pair_score = jnp.einsum(
        "pf,pf->p", head_rows, tail_rows, preferred_element_type=jnp.float32
    ) / math.sqrt(feature_width)
    is_positive = (jnp.arange(pair_total) < pair_total // 5).astype(jnp.float32)
    grad_score = (jax.nn.sigmoid(pair_score) - is_positive) * (master_rows / (2.0 * pair_total))
    partial_value = jnp.zeros((mirror.shape[0], feature_width), jnp.float32)
    partial_value = partial_value.at[node_a].add(grad_score[:, None] * tail_rows)
    partial_value = partial_value.at[node_b].add(grad_score[:, None] * head_rows)
    hidden_grad = lax.psum_scatter(partial_value, "dev", scatter_dimension=0, tiled=True)
    pre_grad = act_back(hidden_grad)[0].astype(jnp.bfloat16)
    weight_terms = jnp.einsum(
        "rf,rg->fg", node_aggregate, pre_grad, preferred_element_type=jnp.float32
    )
    weight_grad = lax.psum(weight_terms, ("group", "dev"))
    agg_grad = jnp.einsum("rg,fg->rf", pre_grad, weight, preferred_element_type=jnp.float32).astype(
        jnp.bfloat16
    )
    dst_rows = lax.all_gather(agg_grad, "group", axis=0, tiled=True)
    dst_blocks = dst_rows.reshape(-1, tile_size, feature_width)[tile_dst]
    tile_terms = jnp.einsum("sij,sjf->sif", tiles, dst_blocks, preferred_element_type=jnp.float32)
    live_mask = (jnp.arange(tiles.shape[0]) < tile_count[0]).astype(jnp.float32)
    tile_terms = tile_terms * live_mask[:, None, None]
    source_part = jnp.zeros((mirror.shape[0] // tile_size, tile_size, feature_width), jnp.float32)
    source_part = source_part.at[tile_src].add(tile_terms).reshape(mirror.shape[0], feature_width)
    feature_grad = lax.psum_scatter(source_part, "dev", scatter_dimension=0, tiled=True).astype(
        jnp.bfloat16
    )
    return (feature_grad, weight_grad)


def solution(mesh):
    return jax.shard_map(
        per_device,
        mesh=mesh,
        in_specs=(
            P(("group", "dev"), None),
            P(),
            P(("group", "dev"), None, None),
            P(("group", "dev")),
            P(("group", "dev")),
            P(("group", "dev")),
            P(("group", "dev"), None),
            P(("group", "dev"), None),
        ),
        out_specs=(P(("group", "dev"), None), P()),
        check_vma=False,
    )
```

profile of v0, /device:TPU:2, one launch (start us, length us, event | category | flops | bytes accessed | tf_op | source)
XLA Modules:
  0.0 871.1 jit_solution(17047929012476843914)
XLA Ops:
  7.2 0.0 copy-start
  7.2 0.0 all-gather.2.cloned.1.call-start
  7.2 2.0 multiply_convert_fusion
  9.2 0.0 all-gather.2.cloned.1.call-update
  9.3 0.0 reduce-scatter.3.cloned.1.call-start
  9.3 1.1 compare_select_fusion
  10.4 83.0 %all-gather.2.cloned.1.call-done = bf16[4096,512]{1,0:T(8,128)(2,1)} async-done(((bf16[64,512]{1,0:T(8,128)(2,1)}), bf16[4096,512]{1,0:T(8,128)(2,1)}) %all-gather.2.cloned.1.call-update) | async-done | bytes 4194320 | tf_op jit(solution)/shard_map/all_gather | solution.py:18
  93.4 36.5 %gather_fusion = bf16[8192,512]{1,0:T(8,128)(2,1)} fusion(bf16[4096,512]{1,0:T(8,128)(2,1)} %all-gather.2.cloned.1.call-done, s32[8192]{0:T(1024)S(1)} %broadcast_clamp_fusion.1), kind=kCustom, calls=%fused_computation | custom fusion | bytes 16809984 | tf_op jit(solution)/shard_map/gather | solution.py:22
  129.9 36.5 %gather_fusion.1 = bf16[8192,512]{1,0:T(8,128)(2,1)} fusion(bf16[4096,512]{1,0:T(8,128)(2,1)} %all-gather.2.cloned.1.call-done, s32[8192]{0:T(1024)S(1)} %broadcast_clamp_fusion), kind=kCustom, calls=%fused_computation.1 | custom fusion | bytes 16809984 | tf_op jit(solution)/shard_map/gather | solution.py:23
  166.4 8.0 fusion.1
  174.5 56.9 %scatter_custom_fusion = f32[4096,512]{1,0:T(8,128)} fusion(s32[8192]{0:T(1024)S(1)} %bitcast.23, bf16[8192,512]{1,0:T(8,128)(2,1)} %gather_fusion.1, f32[8192]{0:T(1024)S(1)} %subtract_multiply_fusion, f32[]{:T(128)} %constant.15.clone.1), kind=kCustom, calls=%fused_computation.9 | custom fusion | flops 12582912 | bytes 16809988 | tf_op jit(solution)/shard_map/scatter-add | solution.py:30
  231.3 59.7 %scatter_custom_fusion.1 = f32[4096,512]{1,0:T(8,128)} fusion(f32[4096,512]{1,0:T(8,128)} %scatter_custom_fusion, s32[8192]{0:T(1024)S(1)} %bitcast.21, bf16[8192,512]{1,0:T(8,128)(2,1)} %gather_fusion, f32[8192]{0:T(1024)S(1)} %subtract_multiply_fusion), kind=kCustom, calls=%fused_computation.11 | custom fusion | flops 12582912 | bytes 16809984 | tf_op jit(solution)/shard_map/scatter-add | solution.py:31
  291.1 0.0 copy-start.3
  291.1 0.0 copy-start.4
  291.1 0.0 copy-start.1
  291.1 0.0 copy-start.2
  291.1 0.0 reduce-scatter.3.cloned.1.call-update
  291.1 0.0 all-reduce.2.cloned.1.call-start
  291.9 0.0 copy-done.3
  291.9 0.0 copy-done.4
  291.9 148.3 %reduce-scatter.3.cloned.1.call-done = f32[64,512]{1,0:T(8,128)} async-done(((f32[4096,512]{1,0:T(8,128)}), f32[64,512]{1,0:T(8,128)}) %reduce-scatter.3.cloned.1.call-update) | async-done | bytes 131088 | tf_op jit(solution)/shard_map/reduce_scatter | solution.py:32
  440.2 1.0 fusion.12
  441.2 0.0 copy-done.1
  441.2 0.3 convolution_convert_fusion
  441.5 0.0 copy-done.2
  441.5 1.3 convolution_bitcast_fusion
  442.8 12.3 %all_gather.7 = bf16[256,512]{1,0:T(8,128)(2,1)S(1)} all-gather(bf16[64,512]{1,0:T(8,128)(2,1)S(1)} %convolution_convert_fusion), channel_id=1, replica_groups=mesh['group'=4,'dev'=64] {'group'}, dimensions={0}, use_global_device_ids=true | all-gather | bytes 327680 | tf_op jit(solution)/shard_map/all_gather | solution.py:41
  455.1 0.0 all-reduce.2.cloned.1.call-update
  455.1 0.0 reduce-scatter.5.cloned.1.call-start
  455.1 2.7 gather_fusion.2
  457.9 0.0 copy-done
  457.9 7.0 multiply_bitcast_fusion
  464.9 9.0 %copy.13 = f32[32,128,512]{2,1,0:T(8,128)} copy(f32[32,128,512]{1,2,0:T(8,128)} %multiply_bitcast_fusion) | data formatting | bytes 16777216 | tf_op jit(solution)/shard_map/mul | solution.py:45
  474.0 4.3 broadcast_in_dim.8
  478.2 18.6 %scatter_fusion = f32[32,128,512]{2,1,0:T(8,128)} fusion(f32[32,128,512]{2,1,0:T(8,128)} %broadcast_in_dim.8, s32[32]{0:T(128)S(1)} %compare_select_fusion.3, f32[32,128,512]{2,1,0:T(8,128)} %copy.13), kind=kCustom, calls=%fused_computation.5 | custom fusion | flops 2097152 | bytes 25165952 | tf_op jit(solution)/shard_map/scatter-add | solution.py:47
  496.8 0.0 reduce-scatter.5.cloned.1.call-update
  496.8 212.3 %all-reduce.2.cloned.1.call-done = f32[512,512]{0,1:T(8,128)} async-done(((f32[512,512]{0,1:T(8,128)}), f32[512,512]{0,1:T(8,128)}) %all-reduce.2.cloned.1.call-update) | async-done | bytes 1048592 | tf_op jit(solution)/shard_map/psum | solution.py:37
  709.1 2.5 copy.14
  711.7 151.4 %reduce-scatter.5.cloned.1.call-done = f32[64,512]{1,0:T(8,128)} async-done(((f32[4096,512]{1,0:T(8,128)}), f32[64,512]{1,0:T(8,128)}) %reduce-scatter.5.cloned.1.call-update) | async-done | bytes 131088 | tf_op jit(solution)/shard_map/reduce_scatter | solution.py:48
  863.0 1.5 convert_element_type.35
  (7 shorter events, 0.1 us)
Async XLA Ops:
  7.2 450.7 %copy-start = (bf16[32,128,128]{2,1,0:T(8,128)(2,1)S(1)}, bf16[32,128,128]{2,1,0:T(8,128)(2,1)}, u32[]{:S(2)}) copy-start(bf16[32,128,128]{2,1,0:T(8,128)(2,1)} %param.10) | copy-start | bytes 3145732
  7.2 86.2 %all-gather.2.cloned.1.call-start = ((), (), s32[]{:S(2)}) async-start(), calls=%async_computation.2 | async-start | bytes 4259840 | tf_op jit(solution)/shard_map/all_gather | solution.py:18
  9.3 431.0 %reduce-scatter.3.cloned.1.call-start = ((), (), s32[]{:S(2)}) async-start(), calls=%async_computation.3 | async-start | bytes 8519680 | tf_op jit(solution)/shard_map/reduce_scatter | solution.py:32
  291.1 0.8 copy-start.3
  291.1 0.8 copy-start.4
  291.1 150.2 %copy-start.1 = (bf16[512,512]{1,0:T(8,128)(2,1)S(1)}, bf16[512,512]{1,0:T(8,128)(2,1)}, u32[]{:S(2)}) copy-start(bf16[512,512]{1,0:T(8,128)(2,1)} %param.9) | copy-start | bytes 1572868
  291.1 150.4 %copy-start.2 = (bf16[64,512]{1,0:T(8,128)(2,1)S(1)}, bf16[64,512]{1,0:T(8,128)(2,1)}, u32[]{:S(2)}) copy-start(bf16[64,512]{1,0:T(8,128)(2,1)} %param.8) | copy-start | bytes 196612
  291.1 418.0 %all-reduce.2.cloned.1.call-start = ((), (), s32[]{:S(2)}) async-start(), calls=%async_computation.5 | async-start | bytes 2097152 | tf_op jit(solution)/shard_map/psum | solution.py:37
  455.1 408.0 %reduce-scatter.5.cloned.1.call-start = ((), (), s32[]{:S(2)}) async-start(), calls=%async_computation.4 | async-start | bytes 8519680 | tf_op jit(solution)/shard_map/reduce_scatter | solution.py:48
Sparse Core Ops, SparseCore 0:
  11.4 81.9 all-gather.1
  291.2 148.9 reduce-scatter.2
  455.2 253.8 all-reduce.1
  713.2 149.7 reduce-scatter.4
where the time goes:
time: 872 us; the launch traced here: 871 us
  waiting for transfers between devices  595 us (68%)
  other arithmetic  147 us (17%)
  local copies, waits for them, and re-layouts  91.6 us (11%)
  between operations  14.6 us (2%)
  blocking collectives  12.3 us (1%)
  matrix products  10.6 us (1%)
    psum x1, waiting for transfers between devices, per_device(): weight_grad = lax.psum(weight_terms, ('group', 'dev'))  212 us
    reduce_scatter x1, waiting for transfers between devices, per_device(): lax.psum_scatter(source_part, 'dev', scatter_dimension=0, tiled=True)  151 us
    reduce_scatter x1, waiting for transfers between devices, per_device(): lax.psum_scatter(partial_value, 'dev', scatter_dimension=0, tiled=True)  148 us
    all_gather x1, waiting for transfers between devices, per_device(): mirror = lax.all_gather(hidden_b, 'dev', axis=0, tiled=True)  83 us
    scatter-add x1, other arithmetic, per_device(): partial_value.at[node_b].add(grad_score[:, None] * head_rows)  59.7 us
    scatter-add x1, other arithmetic, per_device(): partial_value.at[node_a].add(grad_score[:, None] * tail_rows)  56.9 us
    gather x1, local copies, waits for them, and re-layouts, per_device(): head_rows = mirror[node_a]  36.5 us
    gather x1, local copies, waits for them, and re-layouts, per_device(): tail_rows = mirror[node_b]  36.5 us
  transfers between devices with their start and end apart: 4, of which 4 were waited for; matrix products, arithmetic and copies ran while one was open for 5% of the time, Pallas kernels for 0%

commit v1 on v0

--- a/solution.py
+++ b/solution.py
@@ -34,7 +34,7 @@
     weight_terms = jnp.einsum(
         "rf,rg->fg", node_aggregate, pre_grad, preferred_element_type=jnp.float32
     )
-    weight_grad = lax.psum(weight_terms, ("group", "dev"))
+    weight_grad = lax.psum(lax.psum(weight_terms, "dev"), "group")
     agg_grad = jnp.einsum("rg,fg->rf", pre_grad, weight, preferred_element_type=jnp.float32).astype(
         jnp.bfloat16
     )

time: 872 us -> 844 us (0.968)
  waiting for transfers between devices: 595 us -> 567 us
    psum x1 -> x2, waiting for transfers between devices: 212 us -> 185 us  [per_device(): weight_grad = lax.psum(lax.psum(weight_terms, 'dev'), 'group')]
  transfers between devices with their start and end apart: 4 -> 5, of which waited for: 4 -> 4; matrix products, arithmetic and copies ran while one was open for 5% -> 5% of each run, Pallas kernels for 0% -> 0%
where the time goes in v1:
time: 844 us; the launch traced here: 843 us
  waiting for transfers between devices  567 us (67%)
  other arithmetic  147 us (17%)
  local copies, waits for them, and re-layouts  91.6 us (11%)
  between operations  14.5 us (2%)
  blocking collectives  12.6 us (1%)
  matrix products  10.7 us (1%)
    psum x2, waiting for transfers between devices, per_device(): weight_grad = lax.psum(lax.psum(weight_terms, 'dev'), 'group')  185 us
    reduce_scatter x1, waiting for transfers between devices, per_device(): lax.psum_scatter(source_part, 'dev', scatter_dimension=0, tiled=True)  150 us
    reduce_scatter x1, waiting for transfers between devices, per_device(): lax.psum_scatter(partial_value, 'dev', scatter_dimension=0, tiled=True)  149 us
    all_gather x1, waiting for transfers between devices, per_device(): mirror = lax.all_gather(hidden_b, 'dev', axis=0, tiled=True)  83 us
    scatter-add x1, other arithmetic, per_device(): partial_value.at[node_b].add(grad_score[:, None] * head_rows)  59.7 us
    scatter-add x1, other arithmetic, per_device(): partial_value.at[node_a].add(grad_score[:, None] * tail_rows)  56.9 us
    gather x1, local copies, waits for them, and re-layouts, per_device(): head_rows = mirror[node_a]  36.5 us
    gather x1, local copies, waits for them, and re-layouts, per_device(): tail_rows = mirror[node_b]  36.5 us
  transfers between devices with their start and end apart: 5, of which 4 were waited for; matrix products, arithmetic and copies ran while one was open for 5% of the time, Pallas kernels for 0%

profile of v1, /device:TPU:2, one launch (start us, length us, event | category | flops | bytes accessed | tf_op | source)
XLA Modules:
  0.0 843.5 jit_solution(12612297751231978974)
XLA Ops:
  7.2 0.0 copy-start
  7.2 0.0 all-gather.2.cloned.1.call-start
  7.2 2.0 multiply_convert_fusion
  9.2 0.0 all-gather.2.cloned.1.call-update
  9.3 0.0 reduce-scatter.3.cloned.1.call-start
  9.3 1.1 compare_select_fusion
  10.4 83.0 %all-gather.2.cloned.1.call-done = bf16[4096,512]{1,0:T(8,128)(2,1)} async-done(((bf16[64,512]{1,0:T(8,128)(2,1)}), bf16[4096,512]{1,0:T(8,128)(2,1)}) %all-gather.2.cloned.1.call-update) | async-done | bytes 4194320 | tf_op jit(solution)/shard_map/all_gather | solution.py:18
  93.4 36.5 %gather_fusion = bf16[8192,512]{1,0:T(8,128)(2,1)} fusion(bf16[4096,512]{1,0:T(8,128)(2,1)} %all-gather.2.cloned.1.call-done, s32[8192]{0:T(1024)S(1)} %broadcast_clamp_fusion.1), kind=kCustom, calls=%fused_computation | custom fusion | bytes 16809984 | tf_op jit(solution)/shard_map/gather | solution.py:22
  129.9 36.5 %gather_fusion.1 = bf16[8192,512]{1,0:T(8,128)(2,1)} fusion(bf16[4096,512]{1,0:T(8,128)(2,1)} %all-gather.2.cloned.1.call-done, s32[8192]{0:T(1024)S(1)} %broadcast_clamp_fusion), kind=kCustom, calls=%fused_computation.1 | custom fusion | bytes 16809984 | tf_op jit(solution)/shard_map/gather | solution.py:23
  166.4 8.0 fusion.1
  174.5 56.9 %scatter_custom_fusion = f32[4096,512]{1,0:T(8,128)} fusion(s32[8192]{0:T(1024)S(1)} %bitcast.23, bf16[8192,512]{1,0:T(8,128)(2,1)} %gather_fusion.1, f32[8192]{0:T(1024)S(1)} %subtract_multiply_fusion, f32[]{:T(128)} %constant.15.clone.1), kind=kCustom, calls=%fused_computation.9 | custom fusion | flops 12582912 | bytes 16809988 | tf_op jit(solution)/shard_map/scatter-add | solution.py:30
  231.3 59.7 %scatter_custom_fusion.1 = f32[4096,512]{1,0:T(8,128)} fusion(f32[4096,512]{1,0:T(8,128)} %scatter_custom_fusion, s32[8192]{0:T(1024)S(1)} %bitcast.21, bf16[8192,512]{1,0:T(8,128)(2,1)} %gather_fusion, f32[8192]{0:T(1024)S(1)} %subtract_multiply_fusion), kind=kCustom, calls=%fused_computation.11 | custom fusion | flops 12582912 | bytes 16809984 | tf_op jit(solution)/shard_map/scatter-add | solution.py:31
  291.1 0.0 copy-start.2
  291.1 0.0 copy-start.3
  291.1 0.0 copy-start.4
  291.1 0.0 copy-start.1
  291.1 0.0 reduce-scatter.3.cloned.1.call-update
  291.1 0.0 all-reduce.3.cloned.1.call-start
  291.1 149.1 %reduce-scatter.3.cloned.1.call-done = f32[64,512]{1,0:T(8,128)} async-done(((f32[4096,512]{1,0:T(8,128)}), f32[64,512]{1,0:T(8,128)}) %reduce-scatter.3.cloned.1.call-update) | async-done | bytes 131088 | tf_op jit(solution)/shard_map/reduce_scatter | solution.py:32
  440.2 1.0 fusion.12
  441.2 0.0 copy-done.2
  441.2 1.3 convolution_bitcast_fusion
  442.5 0.0 all-reduce.3.cloned.1.call-update
  442.5 0.0 all-reduce.5.cloned.1.call-start
  443.2 0.0 copy-done.3
  443.3 0.0 copy-done.4
  443.3 184.8 %all-reduce.3.cloned.1.call-done = f32[512,512]{0,1:T(8,128)} async-done(((f32[512,512]{0,1:T(8,128)}), f32[512,512]{0,1:T(8,128)}) %all-reduce.3.cloned.1.call-update) | async-done | bytes 1048592 | tf_op jit(solution)/shard_map/psum | solution.py:37
  628.1 0.0 all-reduce.5.cloned.1.call-update
  628.1 0.0 reduce-scatter.5.cloned.1.call-start
  628.2 0.0 copy-done.1
  628.2 0.3 convolution_convert_fusion
  628.5 12.6 %all_gather.7 = bf16[256,512]{1,0:T(8,128)(2,1)S(1)} all-gather(bf16[64,512]{1,0:T(8,128)(2,1)S(1)} %convolution_convert_fusion), channel_id=1, replica_groups=mesh['group'=4,'dev'=64] {'group'}, dimensions={0}, use_global_device_ids=true | all-gather | bytes 327680 | tf_op jit(solution)/shard_map/all_gather | solution.py:41
  641.0 2.7 gather_fusion.2
  643.8 0.0 copy-done
  643.8 7.1 multiply_bitcast_fusion
  650.9 9.0 %copy.13 = f32[32,128,512]{2,1,0:T(8,128)} copy(f32[32,128,512]{1,2,0:T(8,128)} %multiply_bitcast_fusion) | data formatting | bytes 16777216 | tf_op jit(solution)/shard_map/mul | solution.py:45
  659.9 4.3 broadcast_in_dim.8
  664.2 18.7 %scatter_fusion = f32[32,128,512]{2,1,0:T(8,128)} fusion(f32[32,128,512]{2,1,0:T(8,128)} %broadcast_in_dim.8, s32[32]{0:T(128)S(1)} %compare_select_fusion.3, f32[32,128,512]{2,1,0:T(8,128)} %copy.13), kind=kCustom, calls=%fused_computation.5 | custom fusion | flops 2097152 | bytes 25165952 | tf_op jit(solution)/shard_map/scatter-add | solution.py:47
  682.9 0.0 reduce-scatter.5.cloned.1.call-update
  682.9 0.0 all-reduce.5.cloned.1.call-done
  682.9 2.5 copy.14
  685.4 150.0 %reduce-scatter.5.cloned.1.call-done = f32[64,512]{1,0:T(8,128)} async-done(((f32[4096,512]{1,0:T(8,128)}), f32[64,512]{1,0:T(8,128)}) %reduce-scatter.5.cloned.1.call-update) | async-done | bytes 131088 | tf_op jit(solution)/shard_map/reduce_scatter | solution.py:48
  835.4 1.5 convert_element_type.35
  (7 shorter events, 0.1 us)
Async XLA Ops:
  7.2 636.6 %copy-start = (bf16[32,128,128]{2,1,0:T(8,128)(2,1)S(1)}, bf16[32,128,128]{2,1,0:T(8,128)(2,1)}, u32[]{:S(2)}) copy-start(bf16[32,128,128]{2,1,0:T(8,128)(2,1)} %param.10) | copy-start | bytes 3145732
  7.2 86.2 %all-gather.2.cloned.1.call-start = ((), (), s32[]{:S(2)}) async-start(), calls=%async_computation.2 | async-start | bytes 4259840 | tf_op jit(solution)/shard_map/all_gather | solution.py:18
  9.3 431.0 %reduce-scatter.3.cloned.1.call-start = ((), (), s32[]{:S(2)}) async-start(), calls=%async_computation.3 | async-start | bytes 8519680 | tf_op jit(solution)/shard_map/reduce_scatter | solution.py:32
  291.1 150.2 %copy-start.2 = (bf16[64,512]{1,0:T(8,128)(2,1)S(1)}, bf16[64,512]{1,0:T(8,128)(2,1)}, u32[]{:S(2)}) copy-start(bf16[64,512]{1,0:T(8,128)(2,1)} %param.8) | copy-start | bytes 196612
  291.1 152.2 %copy-start.3 = (s32[32]{0:T(128)S(1)}, s32[32]{0:T(128)}, u32[]{:S(2)}) copy-start(s32[32]{0:T(128)} %param.12) | copy-start | bytes 388
  291.1 152.2 %copy-start.4 = (s32[32]{0:T(128)S(1)}, s32[32]{0:T(128)}, u32[]{:S(2)}) copy-start(s32[32]{0:T(128)} %param.11) | copy-start | bytes 388
  291.1 337.1 %copy-start.1 = (bf16[512,512]{1,0:T(8,128)(2,1)S(1)}, bf16[512,512]{1,0:T(8,128)(2,1)}, u32[]{:S(2)}) copy-start(bf16[512,512]{1,0:T(8,128)(2,1)} %param.9) | copy-start | bytes 1572868
  291.1 337.0 %all-reduce.3.cloned.1.call-start = ((), (), s32[]{:S(2)}) async-start(), calls=%async_computation.5 | async-start | bytes 2097152 | tf_op jit(solution)/shard_map/psum | solution.py:37
  442.5 240.4 %all-reduce.5.cloned.1.call-start = ((), (), s32[]{:S(2)}) async-start(), calls=%async_computation.6 | async-start | bytes 2097152 | tf_op jit(solution)/shard_map/psum | solution.py:37
  628.1 207.3 %reduce-scatter.5.cloned.1.call-start = ((), (), s32[]{:S(2)}) async-start(), calls=%async_computation.4 | async-start | bytes 8519680 | tf_op jit(solution)/shard_map/reduce_scatter | solution.py:48
Sparse Core Ops, SparseCore 0:
  11.4 81.9 all-gather.1
  291.2 148.9 reduce-scatter.2
  444.6 183.4 all-reduce.2
  630.3 47.6 all-reduce.4
  683.0 152.3 reduce-scatter.4
